TPU v7x, 32 devices: a whole 2x2x4 slice. The times are simulated.
32 devices in a mesh: shot: 2 (over y), freq: 4 (over z), tile: 4 (over x, core).
Axes of the slice: x: 2, y: 2, z: 4, core: 2. Of those that a mesh axis runs over, the one named last changes fastest.
Arguments:
- omega: float32 [8], P('freq'), may hold values from 30 to 150
- wavefields: float32 [4, 2, 8, 1024, 256], P('shot', None, 'freq', 'tile'), parts along dimension 0, may hold values from -2.5 to 2.5
- velocity: float32 [2, 1024, 256], P(None, ('tile', 'freq')), may hold values from 1.5 to 4.5
- eta: float32 [2, 1024, 256], P(None, ('tile', 'freq')), may hold values from 0 to 0.3
Outputs:
- image: float32 [4, 1024, 256], P('shot', ('tile', 'freq')), parts along dimension 0
There are 2 independent parts, one for each index of `shot`. A program takes and returns all parts, laid end to end along the dimension named above; an argument that names none is the same for every part. Nothing has to cross between parts.
All inputs are finite; a program needn't handle non-finite values.
Results may differ from a plain program's by a relative error of at most 0.0001.
Values sent between devices are 32-bit elements; how exact they have to be, the bound alone decides.
A program may use at most 64 MiB of HBM per device.

v0:
```python
import jax
import jax.numpy as jnp
from jax import lax
from jax.sharding import PartitionSpec as P

coeffs = ((1, 1.5), (2, -0.15), (3, 1.0 / 90.0))
centre = -49.0 / 9.0
lateral_scale = 0.5
depth_step = 0.01


def with_halo(cells, sides, width):
    for axis, dim in sides:
        count = lax.axis_size(axis)
        ends = count - 1
        head = lax.slice_in_dim(cells, 0, width, axis=dim)
        tail = lax.slice_in_dim(cells, cells.shape[dim] - width, cells.shape[dim], axis=dim)
        cells = jnp.concatenate(
            [
                lax.ppermute(tail, axis, [(i, (i + 1) % count) for i in range(ends)]),
                cells,
                lax.ppermute(head, axis, [((i + 1) % count, i) for i in range(ends)]),
            ],
            axis=dim,
        )
    return cells


def stencil(padded):
    rows = padded.shape[-2] - 6
    cols = padded.shape[-1] - 6
    core = padded[..., 3 : 3 + rows, 3 : 3 + cols]
    total = 2.0 * centre * core
    for shift, weight in coeffs:
        part = (
            padded[..., 3 + shift : 3 + shift + rows, 3 : 3 + cols]
            + padded[..., 3 - shift : 3 - shift + rows, 3 : 3 + cols]
        )
        part = (
            part
            + padded[..., 3 : 3 + rows, 3 + shift : 3 + shift + cols]
            + padded[..., 3 : 3 + rows, 3 - shift : 3 - shift + cols]
        )
        total = total + weight * part
    return total


def advance(field, lap, vel, eta_d, om):
    signs = jnp.array([-1.0, 1.0], jnp.float32).reshape((2,) + (1,) * (field.ndim - 2))
    real_part, imag_part = (field[:, 0], field[:, 1])
    lap_re, lap_im = (lap[:, 0], lap[:, 1])
    theta = lateral_scale * vel * (1.0 + 2.0 * eta_d) / om
    v_re = real_part - signs * theta * lap_im
    v_im = imag_part + signs * theta * lap_re
    phase = om * depth_step / vel
    cosine = jnp.cos(phase)
    sine = signs * jnp.sin(phase)
    out_re = cosine * v_re - sine * v_im
    out_im = cosine * v_im + sine * v_re
    term = jnp.sum(out_re[0] * out_re[1] + out_im[0] * out_im[1], axis=0)
    return (jnp.stack([out_re, out_im], axis=1), term)


def per_device(omega, wavefields, velocity, eta):
    freq_count = omega.shape[0]
    om = omega.reshape(freq_count, 1, 1)
    field = wavefields
    images = []
    for depth in range(velocity.shape[0]):
        rimmed = with_halo(field, (("tile", 3),), 3)
        padded = jnp.pad(rimmed, ((0, 0), (0, 0), (0, 0), (0, 0), (3, 3)))
        lap = stencil(padded)
        vel, eta_d = (
            lax.all_gather(velocity[depth], "freq", axis=0, tiled=True),
            lax.all_gather(eta[depth], "freq", axis=0, tiled=True),
        )
        field, term = advance(field, lap, vel, eta_d, om)
        images.append(lax.psum_scatter(term, "freq", scatter_dimension=0, tiled=True))
    return jnp.stack(images)


def solution(mesh):
    return jax.shard_map(
        per_device,
        mesh=mesh,
        in_specs=(
            P("freq"),
            P("shot", None, "freq", "tile", None),
            P(None, ("tile", "freq"), None),
            P(None, ("tile", "freq"), None),
        ),
        out_specs=P("shot", ("tile", "freq"), None),
        check_vma=False,
    )
```

profile of v0, /device:TPU:0, one launch (start us, length us, event | category | flops | bytes accessed | tf_op | source)
XLA Modules:
  0.0 145.5 jit_solution(230321352615536012)
XLA Ops:
  6.5 0.0 copy-start.2
  6.5 0.0 reduce-scatter.5.cloned.1.call-start
  6.5 0.9 fusion.46
  7.4 1.3 collective-permute-start
  8.7 3.0 %collective-permute-start.1 = (f32[2,2,2,3,256]{4,3,2,1,0:T(4,128)S(1)}, f32[2,2,2,3,256]{4,3,2,1,0:T(4,128)S(1)}, u32[]{:S(2)}, u32[]{:S(2)}) collective-permute-start(f32[2,2,2,3,256]{4,3,2,1,0:T(4,128)S(1)} %get-tuple-element.13), channel_id=1, source_target_pairs={{0,1},{1,2},{2,3},{4,5},{5,6},{6,7},{8,9},{9,10},{10,11},{12,13},{... | collective-permute-start | bytes 73736 | tf_op jit(solution)/shard_map/ppermute | solution.py:20
  11.8 0.7 broadcast_multiply_fusion
  12.4 0.9 fusion.48
  13.3 0.9 fusion.47
  14.2 16.0 %all-gather = f32[1,256,256]{2,1,0:T(8,128)S(1)} all-gather(f32[1,64,256]{2,1,0:T(8,128)S(1)} %get-tuple-element.20), channel_id=2, replica_groups=mesh['shot'=2,'freq'=4,'tile'=4] {'freq'}, dimensions={1}, use_global_device_ids=true | all-gather | bytes 327680 | tf_op jit(solution)/shard_map/all_gather | solution.py:74
  30.2 13.8 %all-gather.3 = f32[1,256,256]{2,1,0:T(8,128)S(1)} all-gather(f32[1,64,256]{2,1,0:T(8,128)S(1)} %get-tuple-element.18), channel_id=5, replica_groups=mesh['shot'=2,'freq'=4,'tile'=4] {'freq'}, dimensions={1}, use_global_device_ids=true | all-gather | bytes 327680 | tf_op jit(solution)/shard_map/all_gather | solution.py:75
  44.1 14.2 %all-gather.2 = f32[1,256,256]{2,1,0:T(8,128)S(1)} all-gather(f32[1,64,256]{2,1,0:T(8,128)S(1)} %get-tuple-element.21), channel_id=4, replica_groups=mesh['shot'=2,'freq'=4,'tile'=4] {'freq'}, dimensions={1}, use_global_device_ids=true | all-gather | bytes 327680 | tf_op jit(solution)/shard_map/all_gather | solution.py:74
  58.3 13.8 %all-gather.1 = f32[1,256,256]{2,1,0:T(8,128)S(1)} all-gather(f32[1,64,256]{2,1,0:T(8,128)S(1)} %get-tuple-element.19), channel_id=3, replica_groups=mesh['shot'=2,'freq'=4,'tile'=4] {'freq'}, dimensions={1}, use_global_device_ids=true | all-gather | bytes 327680 | tf_op jit(solution)/shard_map/all_gather | solution.py:75
  72.2 0.0 copy-done.2
  72.2 0.0 copy-start
  72.2 0.2 broadcast_divide_fusion
  72.4 3.7 %divide_cosine_fusion.1 = (f32[2,256,256]{2,1,0:T(8,128)S(1)}, f32[2,256,256]{2,1,0:T(8,128)S(1)}, f32[2,256,256]{2,1,0:T(8,128)S(1)}, f32[2,256,256]{2,1,0:T(8,128)S(1)}) fusion(f32[256,256]{1,0:T(8,128)S(1)} %bitcast.100, f32[2]{0:T(128)S(1)} %broadcast_multiply_fusion, f32[256,256]{1,0:T(8,128)S(1)} %bitcast.101), kind=kLoop, calls=%fused_computation.92 | loop fusion | flops 262144 | bytes 2621448 | tf_op jit(solution)/shard_map/cos | solution.py:56
  76.1 0.0 copy-done
  76.1 0.2 constant_dynamic-update-slice_fusion.1
  76.3 0.0 collective-permute-done
  76.4 0.0 collective-permute-done.1
  76.4 1.0 select_maximum_fusion.3
  77.4 0.0 copy-start.1
  77.4 3.0 %fusion.11 = f32[2,2,2,256,256]{4,3,2,1,0:T(8,128)S(1)} fusion(f32[2,2,2,3,256]{4,3,2,1,0:T(4,128)S(1)} %collective-permute-done.1, f32[2,2,2,262,262]{4,3,2,1,0:T(8,128)S(1)} %select_maximum_fusion.3, f32[2,2,2,256,256]{4,3,2,1,0:T(8,128)S(1)} %copy-done, f32[2,2,2,259,256]{4,3,2,1,0:T(8,128)S(1)} %constant_dynamic-update-slice_fusion), kind=kLoop, calls=%fused_computation.27 | loop fusion | flops 9961472 | bytes 23093248 | tf_op jit(solution)/shard_map/add | solution.py:44
  80.4 0.0 copy-done.1
  80.4 0.4 fusion.33
  80.8 0.4 fusion.35
  81.3 1.3 collective-permute-start.3
  82.6 1.5 %collective-permute-start.2 = (f32[2,2,2,3,256]{4,3,2,1,0:T(4,128)S(1)}, f32[2,2,2,3,256]{4,3,2,1,0:T(4,128)S(1)}, u32[]{:S(2)}, u32[]{:S(2)}) collective-permute-start(f32[2,2,2,3,256]{4,3,2,1,0:T(4,128)S(1)} %get-tuple-element.11), channel_id=1, source_target_pairs={{1,0},{2,1},{3,2},{5,4},{6,5},{7,6},{9,8},{10,9},{11,10},{13,12},{... | collective-permute-start | bytes 73736 | tf_op jit(solution)/shard_map/ppermute | solution.py:22
  84.1 0.0 collective-permute-done.3
  84.1 3.5 %collective-permute-done.2 = f32[2,2,2,3,256]{4,3,2,1,0:T(4,128)S(1)} collective-permute-done((f32[2,2,2,3,256]{4,3,2,1,0:T(4,128)S(1)}, f32[2,2,2,3,256]{4,3,2,1,0:T(4,128)S(1)}, u32[]{:S(2)}, u32[]{:S(2)}) %collective-permute-start.2) | collective-permute-done | bytes 24608 | tf_op jit(solution)/shard_map/ppermute | solution.py:22
  87.5 1.0 select_maximum_fusion
  88.6 0.4 pad_maximum_fusion.1
  89.0 2.9 %fusion.4 = f32[2,2,2,256,256]{4,3,2,1,0:T(8,128)S(1)} fusion(f32[2,1,2,256,256]{4,3,2,1,0:T(8,128)S(1)} %fusion.35, f32[2,1,2,256,256]{4,3,2,1,0:T(8,128)S(1)} %fusion.33, f32[2,2,2,262,262]{4,3,2,1,0:T(8,128)S(1)} %select_maximum_fusion, f32[2,2,2,259,256]{4,3,2,1,0:T(8,128)S(1)} %get-tuple-element.9, f32[2,2,2,259,256]{4,3,2,1,0:T(8,128)S(1)} %get-tuple-element.8), kind=kLoop, calls=%fused_computation.20 | loop fusion | flops 8912896 | bytes 29360128 | tf_op jit(solution)/shard_map/add | solution.py:44
  91.9 0.9 fusion.36
  92.8 0.6 fusion.37
  93.4 0.8 fusion.39
  94.3 0.0 reduce-scatter.5.cloned.1.call-update
  94.3 0.0 reduce-scatter.3.cloned.1.call-start
  94.4 0.8 fusion.41
  95.2 0.0 reduce-scatter.3.cloned.1.call-update
  95.2 21.6 %reduce-scatter.5.cloned.1.call-done = f32[64,256]{1,0:T(8,128)} async-done(((f32[256,256]{1,0:T(8,128)}), f32[64,256]{1,0:T(8,128)}) %reduce-scatter.5.cloned.1.call-update) | async-done | bytes 65552 | tf_op jit(solution)/shard_map/reduce_scatter | solution.py:78
  116.8 20.2 %reduce-scatter.3.cloned.1.call-done = f32[64,256]{1,0:T(8,128)} async-done(((f32[256,256]{1,0:T(8,128)}), f32[64,256]{1,0:T(8,128)}) %reduce-scatter.3.cloned.1.call-update) | async-done | bytes 65552 | tf_op jit(solution)/shard_map/reduce_scatter | solution.py:78
  137.1 1.5 %pad_maximum_fusion.3 = f32[2,64,256]{2,1,0:T(8,128)} fusion(f32[1,64,256]{2,1,0:T(8,128)} %bitcast.102, f32[1,64,256]{2,1,0:T(8,128)} %bitcast.103), kind=kLoop, calls=%fused_computation.97 | loop fusion | flops 32768 | bytes 262144 | tf_op jit(solution)/shard_map/stack | solution.py:79
  (4 shorter events, 0.1 us)
Async XLA Ops:
  6.5 65.7 %copy-start.2 = (f32[2]{0:T(128)S(1)}, f32[2]{0:T(128)}, u32[]{:S(2)}) copy-start(f32[2]{0:T(128)} %param.6) | copy-start | bytes 28
  6.5 110.3 %reduce-scatter.5.cloned.1.call-start = ((), (), s32[]{:S(2)}) async-start(), calls=%async_computation.3 | async-start | bytes 327680 | tf_op jit(solution)/shard_map/reduce_scatter | solution.py:78
  7.4 68.9 %collective-permute-start = (f32[2,2,2,3,256]{4,3,2,1,0:T(4,128)S(1)}, f32[2,2,2,3,256]{4,3,2,1,0:T(4,128)S(1)}, u32[]{:S(2)}, u32[]{:S(2)}) collective-permute-start(f32[2,2,2,3,256]{4,3,2,1,0:T(4,128)S(1)} %get-tuple-element.12), channel_id=1, source_target_pairs={{1,0},{2,1},{3,2},{5,4},{6,5},{7,6},{9,8},{10,9},{11,10},{13,12},{... | collective-permute-start | bytes 73736 | tf_op jit(solution)/shard_map/ppermute | solution.py:22
  8.7 67.6 %collective-permute-start.1 = (f32[2,2,2,3,256]{4,3,2,1,0:T(4,128)S(1)}, f32[2,2,2,3,256]{4,3,2,1,0:T(4,128)S(1)}, u32[]{:S(2)}, u32[]{:S(2)}) collective-permute-start(f32[2,2,2,3,256]{4,3,2,1,0:T(4,128)S(1)} %get-tuple-element.13), channel_id=1, source_target_pairs={{0,1},{1,2},{2,3},{4,5},{5,6},{6,7},{8,9},{9,10},{10,11},{12,13},{... | collective-permute-start | bytes 73736 | tf_op jit(solution)/shard_map/ppermute | solution.py:20
  72.2 3.9 %copy-start = (f32[2,2,2,256,256]{4,3,2,1,0:T(8,128)S(1)}, f32[2,2,2,256,256]{4,3,2,1,0:T(8,128)}, u32[]{:S(2)}) copy-start(f32[2,2,2,256,256]{4,3,2,1,0:T(8,128)} %param.7) | copy-start | bytes 6291460
  77.4 3.0 %copy-start.1 = (f32[2]{0:T(128)S(1)}, f32[2]{0:T(128)}, u32[]{:S(2)}) copy-start(f32[2]{0:T(128)} %constant.22.clone) | copy-start | bytes 28
  81.3 2.8 %collective-permute-start.3 = (f32[2,2,2,3,256]{4,3,2,1,0:T(4,128)S(1)}, f32[2,2,2,3,256]{4,3,2,1,0:T(4,128)S(1)}, u32[]{:S(2)}, u32[]{:S(2)}) collective-permute-start(f32[2,2,2,3,256]{4,3,2,1,0:T(4,128)S(1)} %get-tuple-element.10), channel_id=1, source_target_pairs={{0,1},{1,2},{2,3},{4,5},{5,6},{6,7},{8,9},{9,10},{10,11},{12,13},{... | collective-permute-start | bytes 73736 | tf_op jit(solution)/shard_map/ppermute | solution.py:20
  82.6 4.9 %collective-permute-start.2 = (f32[2,2,2,3,256]{4,3,2,1,0:T(4,128)S(1)}, f32[2,2,2,3,256]{4,3,2,1,0:T(4,128)S(1)}, u32[]{:S(2)}, u32[]{:S(2)}) collective-permute-start(f32[2,2,2,3,256]{4,3,2,1,0:T(4,128)S(1)} %get-tuple-element.11), channel_id=1, source_target_pairs={{1,0},{2,1},{3,2},{5,4},{6,5},{7,6},{9,8},{10,9},{11,10},{13,12},{... | collective-permute-start | bytes 73736 | tf_op jit(solution)/shard_map/ppermute | solution.py:22
  94.3 42.8 %reduce-scatter.3.cloned.1.call-start = ((), (), s32[]{:S(2)}) async-start(), calls=%async_computation.2 | async-start | bytes 327680 | tf_op jit(solution)/shard_map/reduce_scatter | solution.py:78
Sparse Core Ops, SparseCore 0:
  94.4 22.3 reduce-scatter.4
  119.2 17.8 reduce-scatter.2
where the time goes:
time: 146 us; the launch traced here: 145 us
  blocking collectives  57.9 us (40%)
  waiting for transfers between devices  45.4 us (31%)
  other arithmetic  18.6 us (13%)
  between operations  13.6 us (9%)
  starting transfers between devices  7.13 us (5%)
  local copies, waits for them, and re-layouts  2.91 us (2%)
    reduce_scatter x2, waiting for transfers between devices, per_device(): lax.psum_scatter(term, 'freq', scatter_dimension=0, tiled=True)  41.9 us
    all_gather x2, blocking collectives, per_device(): lax.all_gather(velocity[depth], 'freq', axis=0, tiled=True)  30.2 us
    all_gather x2, blocking collectives, per_device(): lax.all_gather(eta[depth], 'freq', axis=0, tiled=True)  27.7 us
    add x2, other arithmetic, stencil(): total = total + weight * part  5.84 us
    ppermute x2, starting transfers between devices, with_halo(): lax.ppermute(tail, axis, [(i, (i + 1) % count) for i in range(ends)])  4.32 us
    cos x1, other arithmetic, advance(): cosine = jnp.cos(phase)  3.7 us
    ppermute x2, waiting for transfers between devices, with_halo(): lax.ppermute(head, axis, [((i + 1) % count, i) for i in range(ends)])  3.46 us
  transfers between devices with their start and end apart: 6, of which 3 were waited for; matrix products, arithmetic and copies ran while one was open for 5% of the time, Pallas kernels for 0%

commit v1 on v0

--- a/solution.py
+++ b/solution.py
@@ -1,3 +1,4 @@
+import functools
 import jax
 import jax.numpy as jnp
 from jax import lax
@@ -7,6 +8,36 @@
 centre = -49.0 / 9.0
 lateral_scale = 0.5
 depth_step = 0.01
+
+
+def step_on_pages(frame_in, pos_dim):
+    frame_in = jnp.moveaxis(frame_in, 0, pos_dim)
+    r1 = frame_in.shape
+    return frame_in.reshape(*r1[:pos_dim], r1[pos_dim] * r1[pos_dim + 1], *r1[pos_dim + 2 :])
+
+
+def field_prepare(buf, mesh_name):
+    y = lax.axis_size(mesh_name)
+    s_next = lax.axis_index(mesh_name)
+    finding, part_now = (y, s_next)
+    reached, oldest = (buf[None], 1)
+    while oldest < finding:
+        arr_next = tuple(((d, d ^ oldest) for d in range(finding)))
+        mid_arr = lax.ppermute(reached, mesh_name, arr_next)
+        before = part_now & oldest == 0
+        inter = jnp.where(before, reached, mid_arr)
+        v_next = jnp.where(before, mid_arr, reached)
+        reached = jnp.concatenate([inter, v_next])
+        oldest *= 2
+    return reached
+
+
+def _update_strips_all(frame, payload, axis_no):
+    even = field_prepare(frame, payload)
+    return step_on_pages(even, axis_no)
+
+
+_prepare_skins = functools.partial(_update_strips_all, payload="freq", axis_no=0)
 
 
 def with_halo(cells, sides, width):
@@ -72,7 +103,7 @@
         lap = stencil(padded)
         vel, eta_d = (
             lax.all_gather(velocity[depth], "freq", axis=0, tiled=True),
-            lax.all_gather(eta[depth], "freq", axis=0, tiled=True),
+            _prepare_skins(eta[depth]),
         )
         field, term = advance(field, lap, vel, eta_d, om)
         images.append(lax.psum_scatter(term, "freq", scatter_dimension=0, tiled=True))

time: 146 us -> 136 us (0.932)
  blocking collectives: 57.9 us -> 28.9 us
  starting transfers between devices: 7.13 us -> 13.5 us
  waiting for transfers between devices: 45.4 us -> 50.8 us
  local copies, waits for them, and re-layouts: 2.91 us -> 7.82 us
  other arithmetic: 18.6 us -> 21 us
    all_gather x2 -> x0, blocking collectives: 27.7 us -> none  [per_device(): lax.all_gather(eta[depth], 'freq', axis=0, tiled=True)]
    ppermute x0 -> x4, waiting for transfers between devices: none -> 8.25 us  [field_prepare(): mid_arr = lax.ppermute(reached, mesh_name, arr_next)]
    ppermute x0 -> x4, starting transfers between devices: none -> 6.58 us  [field_prepare(): mid_arr = lax.ppermute(reached, mesh_name, arr_next)]
    unnamed x7 -> x31, local copies, waits for them, and re-layouts: 0.23 us -> 3.81 us
    reduce_scatter x2, waiting for transfers between devices: 41.9 us -> 40 us  [per_device(): lax.psum_scatter(term, 'freq', scatter_dimension=0, tiled=True)]
  transfers between devices with their start and end apart: 6 -> 10, of which waited for: 3 -> 6; matrix products, arithmetic and copies ran while one was open for 5% -> 11% of each run, Pallas kernels for 0% -> 0%
where the time goes in v1:
time: 136 us
  waiting for transfers between devices  50.8 us (37%)
  blocking collectives  28.9 us (21%)
  other arithmetic  21 us (15%)
  between operations  13.7 us (10%)
  starting transfers between devices  13.5 us (10%)
  local copies, waits for them, and re-layouts  7.82 us (6%)
    reduce_scatter x2, waiting for transfers between devices, per_device(): lax.psum_scatter(term, 'freq', scatter_dimension=0, tiled=True)  40 us
    all_gather x2, blocking collectives, per_device(): lax.all_gather(velocity[depth], 'freq', axis=0, tiled=True)  28.9 us
    ppermute x4, waiting for transfers between devices, field_prepare(): mid_arr = lax.ppermute(reached, mesh_name, arr_next)  8.25 us
    ppermute x4, starting transfers between devices, field_prepare(): mid_arr = lax.ppermute(reached, mesh_name, arr_next)  6.58 us
    add x2, other arithmetic, stencil(): total = total + weight * part  5.82 us
    cos x1, other arithmetic, advance(): cosine = jnp.cos(phase)  4.71 us
    ppermute x2, starting transfers between devices, with_halo(): lax.ppermute(tail, axis, [(i, (i + 1) % count) for i in range(ends)])  4.32 us
    unnamed x31, local copies, waits for them, and re-layouts  3.81 us
  transfers between devices with their start and end apart: 10, of which 6 were waited for; matrix products, arithmetic and copies ran while one was open for 11% of the time, Pallas kernels for 0%

profile of v1, /device:TPU:0, one launch (start us, length us, event | category | flops | bytes accessed | tf_op | source)
XLA Modules:
  0.0 135.7 jit_solution(3476796984590326651)
XLA Ops:
  6.5 1.6 %fusion.48 = (f32[2,2,2,3,256]{4,3,2,1,0:T(4,128)}, f32[2,2,2,3,256]{4,3,2,1,0:T(4,128)}) fusion(f32[2,2,2,256,256]{4,3,2,1,0:T(8,128)} %param.7), kind=kLoop, calls=%fused_computation.117 | loop fusion | bytes 98304 | tf_op jit(solution)/shard_map/slice | solution.py:47
  8.2 1.3 collective-permute-start.2
  9.5 3.0 %collective-permute-start.3 = (f32[2,2,2,3,256]{4,3,2,1,0:T(4,128)}, f32[2,2,2,3,256]{4,3,2,1,0:T(4,128)S(1)}, u32[]{:S(2)}, u32[]{:S(2)}) collective-permute-start(f32[2,2,2,3,256]{4,3,2,1,0:T(4,128)} %get-tuple-element.13), channel_id=1, source_target_pairs={{0,1},{1,2},{2,3},{4,5},{5,6},{6,7},{8,9},{9,10},{10,11},{12,13},{... | collective-permute-start | bytes 73736 | tf_op jit(solution)/shard_map/ppermute | solution.py:51
  12.5 0.8 slice.191
  13.4 3.0 %collective-permute-start.4 = (f32[1,64,256]{2,1,0:T(8,128)S(1)}, f32[1,64,256]{2,1,0:T(8,128)}, u32[]{:S(2)}, u32[]{:S(2)}) collective-permute-start(f32[1,64,256]{2,1,0:T(8,128)S(1)} %slice.191), channel_id=1, source_target_pairs={{0,4},{4,0},{8,12},{12,8},{1,5},{5,1},{9,13},{13,9},{2,6},{6,2},{1... | collective-permute-start | bytes 196616 | tf_op jit(solution)/shard_map/ppermute | solution.py:26
  16.4 0.7 broadcast_multiply_fusion
  17.0 0.9 fusion.49
  17.9 14.6 %all-gather = f32[1,256,256]{2,1,0:T(8,128)S(1)} all-gather(f32[1,64,256]{2,1,0:T(8,128)S(1)} %get-tuple-element.27), channel_id=2, replica_groups=mesh['shot'=2,'freq'=4,'tile'=4] {'freq'}, dimensions={1}, use_global_device_ids=true | all-gather | bytes 327680 | tf_op jit(solution)/shard_map/all_gather | solution.py:105
  32.6 14.3 %all-gather.1 = f32[1,256,256]{2,1,0:T(8,128)S(1)} all-gather(f32[1,64,256]{2,1,0:T(8,128)S(1)} %get-tuple-element.28), channel_id=3, replica_groups=mesh['shot'=2,'freq'=4,'tile'=4] {'freq'}, dimensions={1}, use_global_device_ids=true | all-gather | bytes 327680 | tf_op jit(solution)/shard_map/all_gather | solution.py:105
  46.9 0.7 copy-done.10
  47.6 4.7 %divide_cosine_fusion.1 = (f32[2,256,256]{2,1,0:T(8,128)S(1)}, f32[2,256,256]{2,1,0:T(8,128)S(1)}, f32[2,256,256]{2,1,0:T(8,128)}, f32[2,256,256]{2,1,0:T(8,128)}) fusion(f32[256,256]{1,0:T(8,128)S(1)} %bitcast.100, f32[2]{0:T(128)S(1)} %broadcast_multiply_fusion, f32[256,256]{1,0:T(8,128)S(1)} %bitcast.101), kind=kLoop, calls=%fused_computation.92 | loop fusion | flops 262144 | bytes 2621448 | tf_op jit(solution)/shard_map/cos | solution.py:87
  52.3 1.6 %constant_dynamic-update-slice_fusion.1 = f32[2,2,2,259,256]{4,3,2,1,0:T(8,128)} fusion(f32[2,2,2,256,256]{4,3,2,1,0:T(8,128)S(1)} %copy-done), kind=kLoop, calls=%fused_computation.115 | loop fusion | bytes 4194304
  53.9 0.0 collective-permute-done.2
  53.9 0.6 constant_dynamic-update-slice_fusion
  54.5 1.0 select_maximum_fusion.3
  55.6 0.6 copy-done.1
  56.2 2.9 %fusion.11 = f32[2,2,2,256,256]{4,3,2,1,0:T(8,128)S(1)} fusion(f32[2,2,2,3,256]{4,3,2,1,0:T(4,128)S(1)} %collective-permute-done.3, f32[2,2,2,262,262]{4,3,2,1,0:T(8,128)S(1)} %select_maximum_fusion.3, f32[2,2,2,256,256]{4,3,2,1,0:T(8,128)S(1)} %copy-done, f32[2,2,2,259,256]{4,3,2,1,0:T(8,128)S(1)} %copy-done.1), kind=kLoop, calls=%fused_computation.27 | loop fusion | flops 9961472 | bytes 23093248 | tf_op jit(solution)/shard_map/add | solution.py:75
  59.1 0.9 broadcast_select_fusion.5
  60.0 0.3 collective-permute-start
  60.3 0.0 copy-start.14
  60.3 2.5 %collective-permute-start.5 = (f32[2,64,256]{2,1,0:T(8,128)S(1)}, f32[2,64,256]{2,1,0:T(8,128)S(1)}, u32[]{:S(2)}, u32[]{:S(2)}) collective-permute-start(f32[2,64,256]{2,1,0:T(8,128)S(1)} %pad_maximum_fusion.4), channel_id=1, source_target_pairs={{0,8},{4,12},{8,0},{12,4},{1,9},{5,13},{9,1},{13,5},{2,10},{6,14},... | collective-permute-start | bytes 393224 | tf_op jit(solution)/shard_map/ppermute | solution.py:26
  62.8 1.9 %collective-permute-done = f32[1,64,256]{2,1,0:T(8,128)S(1)} collective-permute-done((f32[1,64,256]{2,1,0:T(8,128)S(1)}, f32[1,64,256]{2,1,0:T(8,128)S(1)}, u32[]{:S(2)}, u32[]{:S(2)}) %collective-permute-start) | collective-permute-done | bytes 65568 | tf_op jit(solution)/shard_map/ppermute | solution.py:26
  64.8 0.8 collective-permute-start.1
  65.6 2.8 %collective-permute-done.5 = f32[2,64,256]{2,1,0:T(8,128)S(1)} collective-permute-done((f32[2,64,256]{2,1,0:T(8,128)S(1)}, f32[2,64,256]{2,1,0:T(8,128)S(1)}, u32[]{:S(2)}, u32[]{:S(2)}) %collective-permute-start.5) | collective-permute-done | bytes 131104 | tf_op jit(solution)/shard_map/ppermute | solution.py:26
  68.4 0.0 copy-start.13
  68.5 3.5 %collective-permute-done.1 = f32[2,64,256]{2,1,0:T(8,128)S(1)} collective-permute-done((f32[2,64,256]{2,1,0:T(8,128)S(1)}, f32[2,64,256]{2,1,0:T(8,128)S(1)}, u32[]{:S(2)}, u32[]{:S(2)}) %collective-permute-start.1) | collective-permute-done | bytes 131104 | tf_op jit(solution)/shard_map/ppermute | solution.py:26
  72.1 0.2 broadcast_divide_fusion
  72.3 0.6 fusion.33
  73.0 0.6 fusion.35
  73.6 1.3 collective-permute-start.7
  74.9 1.3 collective-permute-start.6
  76.2 0.0 collective-permute-done.7
  76.2 2.5 %collective-permute-done.6 = f32[2,2,2,3,256]{4,3,2,1,0:T(4,128)S(1)} collective-permute-done((f32[2,2,2,3,256]{4,3,2,1,0:T(4,128)S(1)}, f32[2,2,2,3,256]{4,3,2,1,0:T(4,128)S(1)}, u32[]{:S(2)}, u32[]{:S(2)}) %collective-permute-start.6) | collective-permute-done | bytes 24608 | tf_op jit(solution)/shard_map/ppermute | solution.py:53
  78.7 1.0 select_maximum_fusion
  79.8 0.4 pad_maximum_fusion.1
  80.2 2.9 %fusion.4 = f32[2,2,2,256,256]{4,3,2,1,0:T(8,128)S(1)} fusion(f32[2,1,2,256,256]{4,3,2,1,0:T(8,128)S(1)} %fusion.35, f32[2,1,2,256,256]{4,3,2,1,0:T(8,128)S(1)} %fusion.33, f32[2,2,2,262,262]{4,3,2,1,0:T(8,128)S(1)} %select_maximum_fusion, f32[2,2,2,259,256]{4,3,2,1,0:T(8,128)S(1)} %get-tuple-element.9, f32[2,2,2,259,256]{4,3,2,1,0:T(8,128)S(1)} %get-tuple-element.8), kind=kLoop, calls=%fused_computation.20 | loop fusion | flops 8912896 | bytes 29360128 | tf_op jit(solution)/shard_map/add | solution.py:75
  83.2 1.0 fusion.36
  84.2 0.5 fusion.37
  84.7 0.5 copy-done.2
  85.2 0.8 fusion.39
  86.0 0.0 reduce-scatter.5.cloned.1.call-update
  86.0 0.0 reduce-scatter.3.cloned.1.call-start
  86.1 0.4 copy-done.3
  86.5 0.8 fusion.41
  87.3 0.0 reduce-scatter.3.cloned.1.call-update
  87.4 19.7 %reduce-scatter.5.cloned.1.call-done = f32[64,256]{1,0:T(8,128)} async-done(((f32[256,256]{1,0:T(8,128)}), f32[64,256]{1,0:T(8,128)}) %reduce-scatter.5.cloned.1.call-update) | async-done | bytes 65552 | tf_op jit(solution)/shard_map/reduce_scatter | solution.py:109
  107.1 20.3 %reduce-scatter.3.cloned.1.call-done = f32[64,256]{1,0:T(8,128)} async-done(((f32[256,256]{1,0:T(8,128)}), f32[64,256]{1,0:T(8,128)}) %reduce-scatter.3.cloned.1.call-update) | async-done | bytes 65552 | tf_op jit(solution)/shard_map/reduce_scatter | solution.py:109
  127.4 1.5 %pad_maximum_fusion.5 = f32[2,64,256]{2,1,0:T(8,128)} fusion(f32[1,64,256]{2,1,0:T(8,128)} %bitcast.102, f32[1,64,256]{2,1,0:T(8,128)} %bitcast.103), kind=kLoop, calls=%fused_computation.103 | loop fusion | flops 32768 | bytes 262144 | tf_op jit(solution)/shard_map/stack | solution.py:110
  (37 shorter events, 0.3 us)
Async XLA Ops:
  6.5 45.8 %copy-start = (f32[2,2,2,256,256]{4,3,2,1,0:T(8,128)S(1)}, f32[2,2,2,256,256]{4,3,2,1,0:T(8,128)}, u32[]{:S(2)}) copy-start(f32[2,2,2,256,256]{4,3,2,1,0:T(8,128)} %param.7) | copy-start | bytes 6291460
  6.5 100.5 %reduce-scatter.5.cloned.1.call-start = ((), (), s32[]{:S(2)}) async-start(), calls=%async_computation.3 | async-start | bytes 327680 | tf_op jit(solution)/shard_map/reduce_scatter | solution.py:109
  8.2 45.7 %collective-permute-start.2 = (f32[2,2,2,3,256]{4,3,2,1,0:T(4,128)}, f32[2,2,2,3,256]{4,3,2,1,0:T(4,128)S(1)}, u32[]{:S(2)}, u32[]{:S(2)}) collective-permute-start(f32[2,2,2,3,256]{4,3,2,1,0:T(4,128)} %get-tuple-element.12), channel_id=1, source_target_pairs={{1,0},{2,1},{3,2},{5,4},{6,5},{7,6},{9,8},{10,9},{11,10},{13,12},{... | collective-permute-start | bytes 73736 | tf_op jit(solution)/shard_map/ppermute | solution.py:53
  9.5 45.1 %collective-permute-start.3 = (f32[2,2,2,3,256]{4,3,2,1,0:T(4,128)}, f32[2,2,2,3,256]{4,3,2,1,0:T(4,128)S(1)}, u32[]{:S(2)}, u32[]{:S(2)}) collective-permute-start(f32[2,2,2,3,256]{4,3,2,1,0:T(4,128)} %get-tuple-element.13), channel_id=1, source_target_pairs={{0,1},{1,2},{2,3},{4,5},{5,6},{6,7},{8,9},{9,10},{10,11},{12,13},{... | collective-permute-start | bytes 73736 | tf_op jit(solution)/shard_map/ppermute | solution.py:51
  13.4 45.7 %collective-permute-start.4 = (f32[1,64,256]{2,1,0:T(8,128)S(1)}, f32[1,64,256]{2,1,0:T(8,128)}, u32[]{:S(2)}, u32[]{:S(2)}) collective-permute-start(f32[1,64,256]{2,1,0:T(8,128)S(1)} %slice.191), channel_id=1, source_target_pairs={{0,4},{4,0},{8,12},{12,8},{1,5},{5,1},{9,13},{13,9},{2,6},{6,2},{1... | collective-permute-start | bytes 196616 | tf_op jit(solution)/shard_map/ppermute | solution.py:26
  46.9 0.7 copy-start.10
  52.3 20.7 %copy-start.4 = (f32[2,256,256]{2,1,0:T(8,128)}, f32[2,256,256]{2,1,0:T(8,128)S(1)}, u32[]{:S(2)}) copy-start(f32[2,256,256]{2,1,0:T(8,128)S(1)} %get-tuple-element.14) | copy-start | bytes 1572868
  52.3 20.7 %copy-start.6 = (f32[2,256,256]{2,1,0:T(8,128)}, f32[2,256,256]{2,1,0:T(8,128)S(1)}, u32[]{:S(2)}) copy-start(f32[2,256,256]{2,1,0:T(8,128)S(1)} %get-tuple-element.15) | copy-start | bytes 1572868
  54.5 1.6 %copy-start.1 = (f32[2,2,2,259,256]{4,3,2,1,0:T(8,128)S(1)}, f32[2,2,2,259,256]{4,3,2,1,0:T(8,128)}, u32[]{:S(2)}) copy-start(f32[2,2,2,259,256]{4,3,2,1,0:T(8,128)} %constant_dynamic-update-slice_fusion) | copy-start | bytes 6365188
  56.2 3.0 %copy-start.12 = (f32[2,64,256]{2,1,0:T(8,128)S(1)}, f32[2,64,256]{2,1,0:T(8,128)}, u32[]{:S(2)}) copy-start(f32[2,64,256]{2,1,0:T(8,128)} %param.9) | copy-start | bytes 393220
  59.1 9.3 %copy-start.11 = (f32[1,256,256]{2,1,0:T(8,128)S(1)}, f32[1,256,256]{2,1,0:T(8,128)}, u32[]{:S(2)}) copy-start(f32[1,256,256]{2,1,0:T(8,128)} %copy-done.10) | copy-start | bytes 786436
  60.0 4.7 %collective-permute-start = (f32[1,64,256]{2,1,0:T(8,128)S(1)}, f32[1,64,256]{2,1,0:T(8,128)S(1)}, u32[]{:S(2)}, u32[]{:S(2)}) collective-permute-start(f32[1,64,256]{2,1,0:T(8,128)S(1)} %get-tuple-element.26), channel_id=1, source_target_pairs={{0,4},{4,0},{8,12},{12,8},{1,5},{5,1},{9,13},{13,9},{2,6},{6,2},{1... | collective-permute-start | bytes 196616 | tf_op jit(solution)/shard_map/ppermute | solution.py:26
  60.3 11.8 %copy-start.14 = (f32[2]{0:T(128)S(1)}, f32[2]{0:T(128)}, u32[]{:S(2)}) copy-start(f32[2]{0:T(128)} %param.6) | copy-start | bytes 28
  60.3 8.1 %collective-permute-start.5 = (f32[2,64,256]{2,1,0:T(8,128)S(1)}, f32[2,64,256]{2,1,0:T(8,128)S(1)}, u32[]{:S(2)}, u32[]{:S(2)}) collective-permute-start(f32[2,64,256]{2,1,0:T(8,128)S(1)} %pad_maximum_fusion.4), channel_id=1, source_target_pairs={{0,8},{4,12},{8,0},{12,4},{1,9},{5,13},{9,1},{13,5},{2,10},{6,14},... | collective-permute-start | bytes 393224 | tf_op jit(solution)/shard_map/ppermute | solution.py:26
  64.8 7.2 %collective-permute-start.1 = (f32[2,64,256]{2,1,0:T(8,128)S(1)}, f32[2,64,256]{2,1,0:T(8,128)S(1)}, u32[]{:S(2)}, u32[]{:S(2)}) collective-permute-start(f32[2,64,256]{2,1,0:T(8,128)S(1)} %pad_maximum_fusion.3), channel_id=1, source_target_pairs={{0,8},{4,12},{8,0},{12,4},{1,9},{5,13},{9,1},{13,5},{2,10},{6,14},... | collective-permute-start | bytes 393224 | tf_op jit(solution)/shard_map/ppermute | solution.py:26
  68.4 3.9 %copy-start.13 = (f32[2]{0:T(128)S(1)}, f32[2]{0:T(128)}, u32[]{:S(2)}) copy-start(f32[2]{0:T(128)} %constant.32.clone) | copy-start | bytes 28
  73.6 2.6 %collective-permute-start.7 = (f32[2,2,2,3,256]{4,3,2,1,0:T(4,128)S(1)}, f32[2,2,2,3,256]{4,3,2,1,0:T(4,128)S(1)}, u32[]{:S(2)}, u32[]{:S(2)}) collective-permute-start(f32[2,2,2,3,256]{4,3,2,1,0:T(4,128)S(1)} %get-tuple-element.10), channel_id=1, source_target_pairs={{0,1},{1,2},{2,3},{4,5},{5,6},{6,7},{8,9},{9,10},{10,11},{12,13},{... | collective-permute-start | bytes 73736 | tf_op jit(solution)/shard_map/ppermute | solution.py:51
  74.9 3.8 %collective-permute-start.6 = (f32[2,2,2,3,256]{4,3,2,1,0:T(4,128)S(1)}, f32[2,2,2,3,256]{4,3,2,1,0:T(4,128)S(1)}, u32[]{:S(2)}, u32[]{:S(2)}) collective-permute-start(f32[2,2,2,3,256]{4,3,2,1,0:T(4,128)S(1)} %get-tuple-element.11), channel_id=1, source_target_pairs={{1,0},{2,1},{3,2},{5,4},{6,5},{7,6},{9,8},{10,9},{11,10},{13,12},{... | collective-permute-start | bytes 73736 | tf_op jit(solution)/shard_map/ppermute | solution.py:53
  80.2 2.9 %copy-start.5 = (f32[2,256,256]{2,1,0:T(8,128)S(1)}, f32[2,256,256]{2,1,0:T(8,128)}, u32[]{:S(2)}) copy-start(f32[2,256,256]{2,1,0:T(8,128)} %copy-done.4) | copy-start | bytes 1572868
  80.2 2.9 %copy-start.7 = (f32[2,256,256]{2,1,0:T(8,128)S(1)}, f32[2,256,256]{2,1,0:T(8,128)}, u32[]{:S(2)}) copy-start(f32[2,256,256]{2,1,0:T(8,128)} %copy-done.6) | copy-start | bytes 1572868
  80.2 2.9 %copy-start.8 = (f32[2,256,256]{2,1,0:T(8,128)S(1)}, f32[2,256,256]{2,1,0:T(8,128)}, u32[]{:S(2)}) copy-start(f32[2,256,256]{2,1,0:T(8,128)} %get-tuple-element.31) | copy-start | bytes 1572868
  80.2 2.9 %copy-start.9 = (f32[2,256,256]{2,1,0:T(8,128)S(1)}, f32[2,256,256]{2,1,0:T(8,128)}, u32[]{:S(2)}) copy-start(f32[2,256,256]{2,1,0:T(8,128)} %get-tuple-element.32) | copy-start | bytes 1572868
  84.2 1.0 copy-start.2
  85.2 1.3 copy-start.3
  86.0 41.3 %reduce-scatter.3.cloned.1.call-start = ((), (), s32[]{:S(2)}) async-start(), calls=%async_computation.2 | async-start | bytes 327680 | tf_op jit(solution)/shard_map/reduce_scatter | solution.py:109
Sparse Core Ops, SparseCore 0:
  86.1 20.8 reduce-scatter.4
  109.4 17.8 reduce-scatter.2
